TPU v7x, 32 devices: a whole 2x2x4 slice. The times are simulated.
32 devices in a mesh: sample: 8 (over z, y), span: 2 (over x), kvhead: 2 (over core).
Axes of the slice: x: 2, y: 2, z: 4, core: 2. Of those that a mesh axis runs over, the one named last changes fastest.
Arguments:
- queries: bfloat16 [8, 256, 3584], P('sample', None, 'kvhead'), may hold values from -6 to 6
- outputs: bfloat16 [8, 256, 3584], P('sample', None, 'kvhead'), may hold values from -6 to 6
- grad_out: bfloat16 [8, 256, 3584], P('sample', None, 'kvhead'), may hold values from -48 to 48
- log_norms: float32 [8, 28, 256], P('sample', 'kvhead'), as said below
- lengths: int32 [8], P('sample'), may hold values from 1 to 256, 512 in all
- prompt_key_rows: bfloat16 [2048, 512], P(('sample', 'span'), 'kvhead'), may hold values from -9 to 9
- prompt_value_rows: bfloat16 [2048, 512], P(('sample', 'span'), 'kvhead'), may hold values from -6 to 6
- slice_key_rows: bfloat16 [8, 256, 512], P('sample', 'span', 'kvhead'), may hold values from -9 to 9
- slice_value_rows: bfloat16 [8, 256, 512], P('sample', 'span', 'kvhead'), may hold values from -6 to 6
Outputs:
- grad_queries: bfloat16 [8, 256, 3584], P('sample', 'span', 'kvhead')
- grad_k_prompt: bfloat16 [2048, 512], P(('sample', 'span'), 'kvhead')
- grad_v_prompt: bfloat16 [2048, 512], P(('sample', 'span'), 'kvhead')
- grad_k_self: bfloat16 [8, 256, 512], P('sample', 'span', 'kvhead')
- grad_v_self: bfloat16 [8, 256, 512], P('sample', 'span', 'kvhead')
Inputs may be any that keep to these rules, and one draw needn't show every extreme that they name: `log_norms`: every entry lies between 0.8 and 2.4 above the natural logarithm of 2304.
All inputs are finite; a program needn't handle non-finite values. No bound on the sum of `lengths` on one device may be relied on, other than what follows from the above.
Results may differ from a plain program's by a relative error of at most 0.0051.
Values may be sent and summed in bfloat16 or wider, within the bound.
A program may use at most 64 MiB of HBM per device.

v0:
```python
import math

import jax
import jax.numpy as jnp
from jax import lax
from jax.sharding import PartitionSpec as P

HEAD_WIDTH = 128


def block_size(total_rows, shard_rows):
    block_rows = shard_rows
    while block_rows * 2 <= 512 and total_rows % (block_rows * 2) == 0:
        block_rows = block_rows * 2
    return block_rows


def divide_heads(matrix, head_count):
    return matrix.reshape(matrix.shape[0], head_count, HEAD_WIDTH).transpose(1, 0, 2)


def join_heads(blocks):
    return blocks.transpose(1, 0, 2).reshape(blocks.shape[1], blocks.shape[0] * HEAD_WIDTH)


def shards(
    queries,
    outputs,
    grad_out,
    log_norms,
    lengths,
    prompt_key_rows,
    prompt_value_rows,
    slice_key_rows,
    slice_value_rows,
):
    slice_rows = queries.shape[1]
    kv_local = prompt_key_rows.shape[1] // HEAD_WIDTH
    query_group_width = queries.shape[2] // HEAD_WIDTH // kv_local
    shard_rows = prompt_key_rows.shape[0]
    score_scale = 1.0 / math.sqrt(HEAD_WIDTH)

    def to_groups(input_array):
        return (
            input_array[0]
            .reshape(slice_rows, kv_local, query_group_width, HEAD_WIDTH)
            .transpose(1, 2, 0, 3)
            .reshape(kv_local, query_group_width * slice_rows, HEAD_WIDTH)
        )

    q_rows = to_groups(queries)
    o_rows = to_groups(outputs)
    row_pos = lax.broadcasted_iota(jnp.int32, (query_group_width * slice_rows,), 0) % slice_rows
    live_rows = row_pos < lengths[0]
    g_rows = jnp.where(live_rows[None, :, None], to_groups(grad_out), jnp.zeros((), jnp.bfloat16))
    row_delta = jnp.sum(g_rows.astype(jnp.float32) * o_rows.astype(jnp.float32), axis=-1)
    per_row_norms = log_norms[0].reshape(kv_local, query_group_width * slice_rows)

    def score_terms(key_heads, value_heads, mask):
        scores = (
            jnp.einsum("gqd,gkd->gqk", q_rows, key_heads, preferred_element_type=jnp.float32)
            * score_scale
        )
        prob_rows = jnp.exp(scores - per_row_norms[:, :, None])
        if mask is not None:
            prob_rows = jnp.where(mask[None], prob_rows, 0.0)
        dprobs = jnp.einsum("gqd,gkd->gqk", g_rows, value_heads, preferred_element_type=jnp.float32)
        score_grads = (prob_rows * (dprobs - row_delta[:, :, None])).astype(jnp.bfloat16)
        return (prob_rows.astype(jnp.bfloat16), score_grads)

    def query_term(key_heads, score_grads):
        return (
            jnp.einsum("gqk,gkd->gqd", score_grads, key_heads, preferred_element_type=jnp.float32)
            * score_scale
        )

    def key_terms(prob_low, score_grads):
        key_grad = (
            jnp.einsum("gqk,gqd->gkd", score_grads, q_rows, preferred_element_type=jnp.float32)
            * score_scale
        )
        value_grad = jnp.einsum(
            "gqk,gqd->gkd", prob_low, g_rows, preferred_element_type=jnp.float32
        )
        return (join_heads(key_grad), join_heads(value_grad))

    query_zero = jnp.zeros((kv_local, query_group_width * slice_rows, HEAD_WIDTH), jnp.float32)
    gathered = (
        lax.all_gather(prompt_key_rows, "sample", axis=0, tiled=True),
        lax.all_gather(prompt_value_rows, "sample", axis=0, tiled=True),
    )
    total_keys = gathered[0].shape[0]
    block_rows = block_size(total_keys, shard_rows)

    def query_step(step_index, query_acc):
        offset = step_index * block_rows
        key_heads = divide_heads(
            lax.dynamic_slice_in_dim(gathered[0], offset, block_rows, 0), kv_local
        )
        value_heads = divide_heads(
            lax.dynamic_slice_in_dim(gathered[1], offset, block_rows, 0), kv_local
        )
        prob_low, score_grads = score_terms(key_heads, value_heads, None)
        return query_acc + query_term(key_heads, score_grads)

    query_prompt = lax.fori_loop(0, total_keys // block_rows, query_step, query_zero)
    inner_rows = block_size(lax.axis_size("sample") * shard_rows, shard_rows)

    def key_step(step_index, state):
        offset = step_index * inner_rows
        key_heads = divide_heads(
            lax.dynamic_slice_in_dim(gathered[0], offset, inner_rows, 0), kv_local
        )
        value_heads = divide_heads(
            lax.dynamic_slice_in_dim(gathered[1], offset, inner_rows, 0), kv_local
        )
        prob_low, score_grads = score_terms(key_heads, value_heads, None)
        key_block, value_block = key_terms(prob_low, score_grads)
        return lax.dynamic_update_slice_in_dim(
            state, jnp.concatenate([key_block, value_block], axis=1), offset, 0
        )

    both_grads = lax.psum_scatter(
        lax.fori_loop(
            0,
            lax.axis_size("sample") * shard_rows // inner_rows,
            key_step,
            jnp.zeros(
                (lax.axis_size("sample") * shard_rows, 2 * kv_local * HEAD_WIDTH), jnp.float32
            ),
        ),
        "sample",
        scatter_dimension=0,
        tiled=True,
    )
    key_prompt = both_grads[:, : kv_local * HEAD_WIDTH]
    value_prompt = both_grads[:, kv_local * HEAD_WIDTH :]
    self_rows = slice_key_rows.shape[1]
    col_pos = lax.axis_index("span") * self_rows + lax.broadcasted_iota(jnp.int32, (self_rows,), 0)
    visible_mask = col_pos[None, :] <= row_pos[:, None]
    slice_keys = divide_heads(slice_key_rows[0], kv_local)
    slice_values = divide_heads(slice_value_rows[0], kv_local)
    self_prob, self_grads = score_terms(slice_keys, slice_values, visible_mask)
    slice_query_rows = query_term(slice_keys, self_grads)
    slice_key_gradient, slice_value_gradient = key_terms(self_prob, self_grads)
    query_total = query_prompt + slice_query_rows
    flattened_query = (
        query_total.reshape(kv_local, query_group_width, slice_rows, HEAD_WIDTH)
        .transpose(2, 0, 1, 3)
        .reshape(slice_rows, kv_local * query_group_width * HEAD_WIDTH)
    )
    grad_query = lax.psum_scatter(flattened_query, "span", scatter_dimension=0, tiled=True).astype(
        jnp.bfloat16
    )
    return (
        grad_query[None],
        key_prompt.astype(jnp.bfloat16),
        value_prompt.astype(jnp.bfloat16),
        slice_key_gradient.astype(jnp.bfloat16)[None],
        slice_value_gradient.astype(jnp.bfloat16)[None],
    )


def solution(mesh):
    in_specs = (
        P("sample", None, "kvhead"),
        P("sample", None, "kvhead"),
        P("sample", None, "kvhead"),
        P("sample", "kvhead", None),
        P("sample"),
        P(("sample", "span"), "kvhead"),
        P(("sample", "span"), "kvhead"),
        P("sample", "span", "kvhead"),
        P("sample", "span", "kvhead"),
    )
    out_specs = (
        P("sample", "span", "kvhead"),
        P(("sample", "span"), "kvhead"),
        P(("sample", "span"), "kvhead"),
        P("sample", "span", "kvhead"),
        P("sample", "span", "kvhead"),
    )
    return jax.shard_map(shards, mesh=mesh, in_specs=in_specs, out_specs=out_specs, check_vma=False)
```

profile of v0, /device:TPU:0, one launch (start us, length us, event | category | flops | bytes accessed | tf_op | source)
XLA Modules:
  0.0 229.3 jit_solution(16332947071129689347)
XLA Ops:
  8.0 0.7 copy.88
  8.7 0.8 reduce.1
  9.5 0.9 reshape_squeeze.15
  10.4 1.0 copy.81
  11.3 1.0 copy.84
  12.3 0.9 reshape_squeeze.16
  13.2 29.5 %all_gather.7 = bf16[1024,256]{0,1:T(8,128)(2,1)S(1)} all-gather(bf16[128,256]{0,1:T(8,128)(2,1)S(1)} %copy.84), channel_id=1, replica_groups=mesh['sample'=8,'span'=2,'kvhead'=2] {'sample'}, dimensions={0}, use_global_device_ids=true | all-gather | bytes 589824 | tf_op jit(solution)/shard_map/all_gather | solution.py:90
  42.7 28.7 %all_gather.6 = bf16[1024,256]{0,1:T(8,128)(2,1)} all-gather(bf16[128,256]{0,1:T(8,128)(2,1)S(1)} %copy.81), channel_id=1, replica_groups=mesh['sample'=8,'span'=2,'kvhead'=2] {'sample'}, dimensions={0}, use_global_device_ids=true | all-gather | bytes 589824 | tf_op jit(solution)/shard_map/all_gather | solution.py:89
  72.0 0.6 copy.83
  72.6 1.3 copy.87
  73.9 1.5 copy.85
  75.4 0.6 copy.86
  76.0 1.5 fusion.27
  77.8 25.8 %while.30 = (s32[]{:T(128)}, f32[2,1792,128]{2,1,0:T(8,128)}, bf16[1024,256]{0,1:T(8,128)(2,1)}, bf16[2,1792,128]{2,1,0:T(8,128)(2,1)S(1)}, f32[1,14,256]{2,1,0:...) while((s32[]{:T(128)}, f32[2,1792,128]{2,1,0:T(8,128)}, ...), condition=%wide.wide.region_2.3_spmd.clone, body=%wide.wide.region_1.2_spmd.clone.sunk | while | flops 1419837440 | bytes 23097536 | solution.py:106
  77.8 1.0 constant_dynamic-slice_fusion.9
  79.2 4.1 %fusion.105 = f32[2,512,1792]{2,1,0:T(8,128)} fusion(bf16[2,1792,128]{2,1,0:T(8,128)(2,1)S(1)} %get-tuple-element.649, bf16[512,2,128]{2,0,1:T(8,128)(2,1)S(1)} %copy.135), kind=kOutput, calls=%fused_computation.22.clone.clone.1 | convolution fusion | flops 469762048 | bytes 8519680 | tf_op jit(solution)/shard_map/while/body/eval_jaxpr/gqd,gkd->gqk/dot_general | solution.py:61
  83.3 7.2 %fusion.106 = f32[2,1792,128]{2,1,0:T(8,128)} fusion(f32[2,1792,128]{2,1,0:T(8,128)} %get-tuple-element.634, f32[2,512,1792]{2,1,0:T(8,128)} %fusion.105, bf16[2,1792,128]{2,1,0:T(8,128)(2,1)S(1)} %get-tuple-element.652, f32[2,1792]{1,0:T(2,128)S(1)} %get-tuple-element.653, f32[2,1792]{1,0:T(2,128)S(1)} %get-tuple-element.654, ...), kind=kOutput, calls=%fused_computation.19.clone.clone.1 | convolution fusion | flops 950075392 | bytes 12480513 | tf_op jit(solution)/shard_map/while/body/eval_jaxpr/gqk,gkd->gqd/dot_general | solution.py:73
  90.5 1.0 constant_dynamic-slice_fusion.9
  91.8 4.1 %fusion.105 = f32[2,512,1792]{2,1,0:T(8,128)} fusion(bf16[2,1792,128]{2,1,0:T(8,128)(2,1)S(1)} %get-tuple-element.649, bf16[512,2,128]{2,0,1:T(8,128)(2,1)S(1)} %copy.135), kind=kOutput, calls=%fused_computation.22.clone.clone.1 | convolution fusion | flops 469762048 | bytes 8519680 | tf_op jit(solution)/shard_map/while/body/eval_jaxpr/gqd,gkd->gqk/dot_general | solution.py:61
  95.9 7.7 %fusion.106 = f32[2,1792,128]{2,1,0:T(8,128)} fusion(f32[2,1792,128]{2,1,0:T(8,128)} %get-tuple-element.634, f32[2,512,1792]{2,1,0:T(8,128)} %fusion.105, bf16[2,1792,128]{2,1,0:T(8,128)(2,1)S(1)} %get-tuple-element.652, f32[2,1792]{1,0:T(2,128)S(1)} %get-tuple-element.653, f32[2,1792]{1,0:T(2,128)S(1)} %get-tuple-element.654, ...), kind=kOutput, calls=%fused_computation.19.clone.clone.1 | convolution fusion | flops 950075392 | bytes 12480513 | tf_op jit(solution)/shard_map/while/body/eval_jaxpr/gqk,gkd->gqd/dot_general | solution.py:73
  103.9 0.7 fusion.24
  104.6 0.6 fusion.25
  105.2 1.9 copy-done.5
  107.1 1.6 fusion.20
  108.7 2.8 %copy.91 = f32[2,7,256,128]{2,3,1,0:T(8,128)} copy(f32[2,7,256,128]{3,2,1,0:T(8,128)} %bitcast.141) | data formatting | bytes 3670016 | tf_op jit(solution)/shard_map/reshape | solution.py:148
  111.8 1.3 copy.92
  113.1 1.3 copy.94
  114.4 1.7 broadcast_in_dim.55.clone
  116.0 38.5 %while.29 = (s32[]{:T(128)}, f32[1024,512]{1,0:T(8,128)}, bf16[1024,256]{0,1:T(8,128)(2,1)}, bf16[2,1792,128]{1,2,0:T(8,128)(2,1)}, f32[1,14,256]{2,1,0:T(8,128)...) while((s32[]{:T(128)}, f32[1024,512]{1,0:T(8,128)}, ...), condition=%wide.wide.region_5.6_spmd, body=%wide.wide.region_4.5_spmd.sunk | while | flops 1894121472 | bytes 35809516 | solution.py:124
  116.0 1.0 constant_dynamic-slice_fusion.8
  117.4 5.2 %fusion.97 = f32[2,512,1792]{2,1,0:T(8,128)} fusion(bf16[2,1792,128]{1,2,0:T(8,128)(2,1)} %get-tuple-element.688, bf16[512,2,128]{2,0,1:T(8,128)(2,1)S(1)} %copy.132), kind=kOutput, calls=%fused_computation.10.clone.clone.1 | convolution fusion | flops 469762048 | bytes 8519680 | tf_op jit(solution)/shard_map/while/body/eval_jaxpr/gqd,gkd->gqk/dot_general | solution.py:61
  122.6 6.4 %fusion.99 = f32[2,512,128]{1,2,0:T(8,128)S(1)} fusion(bf16[2,1792,128]{1,2,0:T(8,128)(2,1)} %get-tuple-element.688, f32[2,512,1792]{2,1,0:T(8,128)} %fusion.97, bf16[2,1792,128]{1,2,0:T(8,128)(2,1)} %get-tuple-element.691, f32[2,1792]{1,0:T(2,128)S(1)} %get-tuple-element.692, f32[2,1792]{1,0:T(2,128)S(1)} %get-tuple-element.693, ...), kind=kOutput, calls=%fused_computation.7.clone.clone.1 | convolution fusion | flops 948830208 | bytes 9990144 | tf_op jit(solution)/shard_map/while/body/eval_jaxpr/gqk,gqd->gkd/dot_general | solution.py:79
  129.0 4.8 %fusion.98 = f32[2,512,128]{1,2,0:T(8,128)S(1)} fusion(bf16[2,1792,128]{1,2,0:T(8,128)(2,1)} %get-tuple-element.691, f32[2,512,1792]{2,1,0:T(8,128)} %fusion.97, f32[2,1792]{1,0:T(2,128)S(1)} %get-tuple-element.693), kind=kOutput, calls=%fused_computation.3.clone.clone.1 | convolution fusion | flops 475267072 | bytes 8796160 | tf_op jit(solution)/shard_map/while/body/eval_jaxpr/gqk,gqd->gkd/dot_general | solution.py:82
  134.2 1.1 constant_dynamic-update-slice_fusion.3
  135.3 1.0 constant_dynamic-slice_fusion.8
  136.7 5.2 %fusion.97 = f32[2,512,1792]{2,1,0:T(8,128)} fusion(bf16[2,1792,128]{1,2,0:T(8,128)(2,1)} %get-tuple-element.688, bf16[512,2,128]{2,0,1:T(8,128)(2,1)S(1)} %copy.132), kind=kOutput, calls=%fused_computation.10.clone.clone.1 | convolution fusion | flops 469762048 | bytes 8519680 | tf_op jit(solution)/shard_map/while/body/eval_jaxpr/gqd,gkd->gqk/dot_general | solution.py:61
  141.9 6.3 %fusion.99 = f32[2,512,128]{1,2,0:T(8,128)S(1)} fusion(bf16[2,1792,128]{1,2,0:T(8,128)(2,1)} %get-tuple-element.688, f32[2,512,1792]{2,1,0:T(8,128)} %fusion.97, bf16[2,1792,128]{1,2,0:T(8,128)(2,1)} %get-tuple-element.691, f32[2,1792]{1,0:T(2,128)S(1)} %get-tuple-element.692, f32[2,1792]{1,0:T(2,128)S(1)} %get-tuple-element.693, ...), kind=kOutput, calls=%fused_computation.7.clone.clone.1 | convolution fusion | flops 948830208 | bytes 9990144 | tf_op jit(solution)/shard_map/while/body/eval_jaxpr/gqk,gqd->gkd/dot_general | solution.py:79
  148.2 4.8 %fusion.98 = f32[2,512,128]{1,2,0:T(8,128)S(1)} fusion(bf16[2,1792,128]{1,2,0:T(8,128)(2,1)} %get-tuple-element.691, f32[2,512,1792]{2,1,0:T(8,128)} %fusion.97, f32[2,1792]{1,0:T(2,128)S(1)} %get-tuple-element.693), kind=kOutput, calls=%fused_computation.3.clone.clone.1 | convolution fusion | flops 475267072 | bytes 8796160 | tf_op jit(solution)/shard_map/while/body/eval_jaxpr/gqk,gqd->gkd/dot_general | solution.py:82
  153.4 1.1 constant_dynamic-update-slice_fusion.3
  154.5 1.2 copy-done.1
  155.7 1.9 convolution_convert_fusion
  157.7 0.7 copy.100
  158.9 0.7 copy.99
  159.6 1.3 convert_bitcast_fusion.1
  160.9 1.0 copy.98
  161.9 59.0 %reduce-scatter.5.cloned.1.call-done = f32[128,512]{1,0:T(8,128)} async-done(((f32[1024,512]{1,0:T(8,128)}), f32[128,512]{1,0:T(8,128)}) %reduce-scatter.5.cloned.1.call-update) | async-done | bytes 262160 | tf_op jit(solution)/shard_map/reduce_scatter | solution.py:123
  220.8 1.0 convert.12
  221.8 0.7 fusion.43
  (56 shorter events, 4.2 us)
Async XLA Ops:
  7.2 64.3 %copy-start.6 = (bf16[1,256,1792]{2,1,0:T(8,128)(2,1)S(1)}, bf16[1,256,1792]{2,1,0:T(8,128)(2,1)}, u32[]{:S(2)}) copy-start(bf16[1,256,1792]{2,1,0:T(8,128)(2,1)} %param.13) | copy-start | bytes 2752516
  7.2 152.4 %reduce-scatter.3.cloned.1.call-start = ((), (), s32[]{:S(2)}) async-start(), calls=%async_computation.2 | async-start | bytes 2752512 | tf_op jit(solution)/shard_map/reduce_scatter | solution.py:152
  8.7 63.9 %copy-start.8 = (f32[1,14,256]{2,1,0:T(8,128)}, f32[1,14,256]{2,1,0:T(8,128)S(1)}, u32[]{:S(2)}) copy-start(f32[1,14,256]{2,1,0:T(8,128)S(1)} %copy.88) | copy-start | bytes 43012
  42.7 29.9 %copy-start.7 = (bf16[1,256,1792]{2,1,0:T(8,128)(2,1)S(1)}, bf16[1,256,1792]{2,1,0:T(8,128)(2,1)}, u32[]{:S(2)}) copy-start(bf16[1,256,1792]{2,1,0:T(8,128)(2,1)} %param.14) | copy-start | bytes 2752516
  103.6 9.5 %copy-start = (bf16[2,1792,128]{2,1,0:T(8,128)(2,1)}, bf16[2,1792,128]{2,1,0:T(8,128)(2,1)S(1)}, u32[]{:S(2)}) copy-start(bf16[2,1792,128]{2,1,0:T(8,128)(2,1)S(1)} %get-tuple-element.702) | copy-start | bytes 2752516
  104.6 4.1 %copy-start.4 = (f32[2,1792,128]{2,1,0:T(8,128)}, f32[2,1792,128]{2,1,0:T(8,128)S(1)}, u32[]{:S(2)}) copy-start(f32[2,1792,128]{2,1,0:T(8,128)S(1)} %fusion.24) | copy-start | bytes 5505028
  104.6 2.5 %copy-start.5 = (f32[2,1792,128]{2,1,0:T(8,128)S(1)}, f32[2,1792,128]{2,1,0:T(8,128)}, u32[]{:S(2)}) copy-start(f32[2,1792,128]{2,1,0:T(8,128)} %get-tuple-element.283) | copy-start | bytes 5505028
  105.2 3.5 %copy-start.2 = (bf16[2,1792,128]{2,1,0:T(8,128)(2,1)}, bf16[2,1792,128]{2,1,0:T(8,128)(2,1)S(1)}, u32[]{:S(2)}) copy-start(bf16[2,1792,128]{2,1,0:T(8,128)(2,1)S(1)} %fusion.25) | copy-start | bytes 2752516
  108.7 3.0 %copy-start.9 = (f32[1,14,256]{2,1,0:T(8,128)S(1)}, f32[1,14,256]{2,1,0:T(8,128)}, u32[]{:S(2)}) copy-start(f32[1,14,256]{2,1,0:T(8,128)} %get-tuple-element.709) | copy-start | bytes 43012
  111.5 109.3 %reduce-scatter.5.cloned.1.call-start = ((), (), s32[]{:S(2)}) async-start(), calls=%async_computation.3 | async-start | bytes 2359296 | tf_op jit(solution)/shard_map/reduce_scatter | solution.py:123
  116.0 6.6 %copy-start.10 = (f32[2,1792]{1,0:T(2,128)}, f32[2,1792]{1,0:T(2,128)S(1)}, u32[]{:S(2)}) copy-start(f32[2,1792]{1,0:T(2,128)S(1)} %get-tuple-element.692) | copy-start | bytes 43012 | tf_op jit(solution)/shard_map/while
  134.2 1.1 copy-start.11
  135.3 6.6 %copy-start.10 = (f32[2,1792]{1,0:T(2,128)}, f32[2,1792]{1,0:T(2,128)S(1)}, u32[]{:S(2)}) copy-start(f32[2,1792]{1,0:T(2,128)S(1)} %get-tuple-element.692) | copy-start | bytes 43012 | tf_op jit(solution)/shard_map/while
  153.4 1.2 copy-start.11
  154.5 1.2 copy-start.1
  154.5 3.9 %copy-start.3 = (bf16[2,1792,128]{2,1,0:T(8,128)(2,1)S(1)}, bf16[2,1792,128]{2,1,0:T(8,128)(2,1)}, u32[]{:S(2)}) copy-start(bf16[2,1792,128]{2,1,0:T(8,128)(2,1)} %copy-done.2) | copy-start | bytes 2752516
Sparse Core Ops, SparseCore 0:
  111.7 27.0 reduce-scatter.2
  154.7 66.1 reduce-scatter.4
where the time goes:
time: 230 us; the launch traced here: 229 us
  matrix products  60.9 us (26%)
  waiting for transfers between devices  59 us (26%)
  blocking collectives  58.3 us (25%)
  local copies, waits for them, and re-layouts  30.4 us (13%)
  between operations  15 us (7%)
  other arithmetic  5.29 us (2%)
    reduce_scatter x1, waiting for transfers between devices, shards(): lax.psum_scatter(lax.fori_loop(0, lax.axis_size('sample') * shard_rows //...  59 us
    all_gather x1, blocking collectives, shards(): lax.all_gather(prompt_value_rows, 'sample', axis=0, tiled=True)  29.5 us
    all_gather x1, blocking collectives, shards(): lax.all_gather(prompt_key_rows, 'sample', axis=0, tiled=True)  28.7 us
    dot_general x5, matrix products, score_terms(): jnp.einsum('gqd,gkd->gqk', q_rows, key_heads, preferred_element_type=jnp....  19.3 us
    dot_general x3, matrix products, query_term(): jnp.einsum('gqk,gkd->gqd', score_grads, key_heads, preferred_element_type...  16.6 us
    dot_general x3, matrix products, key_terms(): jnp.einsum('gqk,gqd->gkd', score_grads, q_rows, preferred_element_type=jn...  13.1 us
    dot_general x3, matrix products, key_terms(): jnp.einsum('gqk,gqd->gkd', prob_low, g_rows, preferred_element_type=jnp.f...  11.5 us
    unnamed x29, local copies, waits for them, and re-layouts  10.7 us
  transfers between devices with their start and end apart: 2, of which 1 were waited for; matrix products, arithmetic and copies ran while one was open for 21% of the time, Pallas kernels for 0%

commit v1 on v0

v1 whole, which is shorter than its diff:
```python
import functools
import math

import jax
import jax.numpy as jnp
from jax import lax
from jax.experimental import pallas as pl
from jax.experimental.pallas import tpu as pltpu
from jax.sharding import PartitionSpec as P

HEAD_WIDTH = 128
MESH = pl.DeviceIdType.MESH
LOG2E = 1.4426950408889634
F32 = jnp.float32
BF16 = jnp.bfloat16


def dot_nt(a, b):
    return lax.dot_general(a, b, (((1,), (1,)), ((), ())), preferred_element_type=F32)


def dot_nn(a, b):
    return lax.dot_general(a, b, (((1,), (0,)), ((), ())), preferred_element_type=F32)


def dot_tn(a, b):
    return lax.dot_general(a, b, (((0,), (0,)), ((), ())), preferred_element_type=F32)


def kernel(
    n_col, n_span, kv, group,
    len_ref, q_ref, o_ref, g_ref, lse_ref, pk_ref, pv_ref, sk_ref, sv_ref,
    dq_ref, dkp_ref, dvp_ref, dks_ref, dvs_ref,
    qst, gst, lse2, delta, kv_all, probs, grads, dqt, dqf, dqs, dqr,
    own, ysend, yrecv, zsend, zrecv,
    kv_recv, kvz_send, kvy_send, y_ssem, y_rsem, z_ssem, z_rsem, q_ssem, q_rsem,
):
    rows = q_ref.shape[1]
    shard = pk_ref.shape[0]
    width = HEAD_WIDTH
    part = rows // n_span
    scale = 1.0 / math.sqrt(HEAD_WIDTH)
    sample = lax.axis_index("sample")
    span = lax.axis_index("span")
    core = lax.axis_index("kvhead")
    col = sample // 2
    side = sample % 2

    def at_sample(c, y):
        return (c * 2 + y, span, core)

    def column(k):
        return lax.rem(col - k + n_col, n_col)

    partner = at_sample(col, 1 - side)

    barrier = pltpu.get_barrier_semaphore()
    for d in range(1, n_col):
        pl.semaphore_signal(barrier, inc=1, device_id=at_sample(column(d), side), device_id_type=MESH)
    pl.semaphore_signal(barrier, inc=1, device_id=partner, device_id_type=MESH)
    for e in range(1, n_span):
        peer = (sample, lax.rem(span + e, n_span), core)
        pl.semaphore_signal(barrier, inc=1, device_id=peer, device_id_type=MESH)

    for g in range(kv):
        lanes = slice(g * width, (g + 1) * width)
        kv_all[g, sample, :, 0:width] = pk_ref[:, lanes]
        kv_all[g, sample, :, width:2 * width] = pv_ref[:, lanes]
    pl.semaphore_wait(barrier, n_col + n_span - 1)

    def z_copy(g, d):
        return pltpu.make_async_remote_copy(
            src_ref=kv_all.at[g, sample], dst_ref=kv_all.at[g, sample],
            send_sem=kvz_send.at[g, d], recv_sem=kv_recv.at[g, sample],
            device_id=at_sample(lax.rem(col + d, n_col), side), device_id_type=MESH)

    def y_copy(g, k):
        s = column(k) * 2 + side
        return pltpu.make_async_remote_copy(
            src_ref=kv_all.at[g, s], dst_ref=kv_all.at[g, s],
            send_sem=kvy_send.at[g, k], recv_sem=kv_recv.at[g, s],
            device_id=partner, device_id_type=MESH)

    def wait_block(g, s):
        pltpu.make_async_remote_copy(
            src_ref=kv_all.at[g, s], dst_ref=kv_all.at[g, s],
            send_sem=kvy_send.at[g, 0], recv_sem=kv_recv.at[g, s],
            device_id=partner, device_id_type=MESH).wait_recv()

    def forward(g, k):
        wait_block(g, column(k) * 2 + side)
        y_copy(g, k).start()

    def ysum_copy(g, k):
        return pltpu.make_async_remote_copy(
            src_ref=ysend.at[g, k], dst_ref=yrecv.at[g, k],
            send_sem=y_ssem.at[g, k], recv_sem=y_rsem.at[g, k],
            device_id=partner, device_id_type=MESH)

    def zsum_copy(g, k):
        return pltpu.make_async_remote_copy(
            src_ref=zsend.at[g, k], dst_ref=zrecv.at[g, k],
            send_sem=z_ssem.at[g, k], recv_sem=z_rsem.at[g, k],
            device_id=at_sample(column(k), side), device_id_type=MESH)

    def query_copy(g, e):
        other = lax.rem(span + e, n_span)
        return pltpu.make_async_remote_copy(
            src_ref=dqs.at[g, other], dst_ref=dqr.at[g, e],
            send_sem=q_ssem.at[g, e], recv_sem=q_rsem.at[g, e],
            device_id=(sample, other, core), device_id_type=MESH)

    for g in range(kv):
        for d in range(1, n_col):
            z_copy(g, d).start()
        y_copy(g, 0).start()

    live = lax.broadcasted_iota(jnp.int32, (rows, width), 0) < len_ref[0]
    lse2[...] = lse_ref[0] * LOG2E
    for h in range(kv * group):
        lanes = slice(h * width, (h + 1) * width)
        g, i = divmod(h, group)
        span_rows = slice(i * rows, (i + 1) * rows)
        qst[g, span_rows, :] = q_ref[0, :, lanes]
        grad = jnp.where(live, g_ref[0, :, lanes].astype(F32), 0.0)
        gst[g, span_rows, :] = grad.astype(BF16)
        prod = grad * o_ref[0, :, lanes].astype(F32)
        delta[h:h + 1, :] = jnp.sum(prod.T, axis=0, keepdims=True)

    def block(g, keys, values, mask, first):
        count = keys.shape[0]
        for i in range(group):
            h = g * group + i
            span_rows = slice(i * rows, (i + 1) * rows)
            scores = dot_nt(keys, qst[g, span_rows, :])
            prob = jnp.exp2(scores * (scale * LOG2E) - lse2[h:h + 1, :])
            if mask is not None:
                prob = jnp.where(mask, prob, 0.0)
            dprob = dot_nt(values, gst[g, span_rows, :])
            probs[0:count, span_rows] = prob.astype(BF16)
            grads[0:count, span_rows] = (prob * (dprob - delta[h:h + 1, :])).astype(BF16)
        low = grads[0:count, :]
        term = dot_tn(keys, low)
        if first:
            dqt[...] = term
        else:
            dqt[...] += term
        key_grad = dot_nn(low, qst[g]) * scale
        value_grad = dot_nn(probs[0:count, :], gst[g])
        return key_grad, value_grad

    self_rows = sk_ref.shape[1]
    key_pos = span * self_rows + lax.broadcasted_iota(jnp.int32, (self_rows, rows), 0)
    visible = key_pos <= lax.broadcasted_iota(jnp.int32, (self_rows, rows), 1)

    def column_block(g, k):
        c = column(k)
        pair = kv_all[g, pl.ds(c * 2, 2)].reshape(2 * shard, 2 * width)
        key_grad, value_grad = block(g, pair[:, :width], pair[:, width:], None, False)
        own[0, :, 0:width] = key_grad[:shard]
        own[1, :, 0:width] = key_grad[shard:]
        own[0, :, width:] = value_grad[:shard]
        own[1, :, width:] = value_grad[shard:]
        ysend[g, k] = own[1 - side].astype(BF16)
        ysum_copy(g, k).start()
        dqf_own = own[side]
        return dqf_own

    def z_finish(g, k):
        ysum_copy(g, k).wait_recv()
        zsend[g, k] = (zhold[g, k] + yrecv[g, k].astype(F32)).astype(BF16)
        zsum_copy(g, k).start()

    zhold = dqf["hold"]
    dq_acc = dqf["query"]

    for g in range(kv):
        lanes = slice(g * width, (g + 1) * width)
        key_grad, value_grad = block(g, sk_ref[0, :, lanes], sv_ref[0, :, lanes], visible, True)
        dks_ref[0, :, lanes] = key_grad.astype(BF16)
        dvs_ref[0, :, lanes] = value_grad.astype(BF16)
        if g == 0:
            forward(g, 1)

        def step(k, carry, g=g):
            if g == 0:
                @pl.when(k + 1 < n_col)
                def _():
                    forward(g, k + 1)
            wait_block(g, column(k) * 2 + 1 - side)
            zhold[g, k] = column_block(g, k)

            @pl.when(k >= 2)
            def _():
                z_finish(g, k - 1)
            return carry

        lax.fori_loop(1, n_col, step, 0)
        for later in range(1, kv):
            if g == 0:
                for k in range(1, n_col):
                    forward(later, k)
        wait_block(g, column(0) * 2 + 1 - side)
        zhold[g, 0] = column_block(g, 0)
        z_finish(g, n_col - 1)
        for i in range(group):
            lanes_i = slice(i * width, (i + 1) * width)
            part_sum = dqt[:, i * rows:(i + 1) * rows].T * scale
            whole = part_sum.reshape(n_span, part, width)
            dq_acc[g, :, :, lanes_i] = whole
            dqs[g, :, :, lanes_i] = whole.astype(BF16)
        for e in range(1, n_span):
            query_copy(g, e).start()

    for g in range(kv):
        lanes = slice(g * width, (g + 1) * width)
        ysum_copy(g, 0).wait_recv()
        total = zhold[g, 0] + yrecv[g, 0].astype(F32)
        for k in range(1, n_col):
            zsum_copy(g, k).wait_recv()
            total += zrecv[g, k].astype(F32)
        dkp_ref[:, lanes] = total[:, :width].astype(BF16)
        dvp_ref[:, lanes] = total[:, width:].astype(BF16)
        query_total = dq_acc[g, span]
        for e in range(1, n_span):
            query_copy(g, e).wait_recv()
            query_total += dqr[g, e].astype(F32)
        dq_ref[0, :, g * group * width:(g + 1) * group * width] = query_total.astype(BF16)

    for g in range(kv):
        for d in range(1, n_col):
            z_copy(g, d).wait_send()
            zsum_copy(g, d).wait_send()
        for k in range(n_col):
            y_copy(g, k).wait_send()
            ysum_copy(g, k).wait_send()
        for e in range(1, n_span):
            query_copy(g, e).wait_send()


def body(n_col, n_span, kv, group, *refs):
    refs = list(refs)
    fixed = refs[:14]
    (qst, gst, lse2, delta, kv_all, probs, grads, dqt, query, hold) = refs[14:24]
    rest = refs[24:]
    kernel(n_col, n_span, kv, group, *fixed, qst, gst, lse2, delta, kv_all, probs, grads, dqt,
           {"query": query, "hold": hold}, *rest)


def shards(n_sample, n_span, queries, outputs, grad_out, log_norms, lengths,
           prompt_key_rows, prompt_value_rows, slice_key_rows, slice_value_rows):
    rows = queries.shape[1]
    shard = prompt_key_rows.shape[0]
    width = HEAD_WIDTH
    kv = prompt_key_rows.shape[1] // width
    heads = queries.shape[2] // width
    group = heads // kv
    n_col = n_sample // 2
    part = rows // n_span
    vmem = pl.BlockSpec(memory_space=pltpu.VMEM)
    dma = pltpu.SemaphoreType.DMA
    out_shape = (
        jax.ShapeDtypeStruct((1, part, heads * width), BF16),
        jax.ShapeDtypeStruct(prompt_key_rows.shape, BF16),
        jax.ShapeDtypeStruct(prompt_key_rows.shape, BF16),
        jax.ShapeDtypeStruct(slice_key_rows.shape, BF16),
        jax.ShapeDtypeStruct(slice_key_rows.shape, BF16),
    )
    scratch = [
        pltpu.VMEM((kv, group * rows, width), BF16),
        pltpu.VMEM((kv, group * rows, width), BF16),
        pltpu.VMEM((heads, rows), F32),
        pltpu.VMEM((heads, rows), F32),
        pltpu.VMEM((kv, n_sample, shard, 2 * width), BF16),
        pltpu.VMEM((2 * shard, group * rows), BF16),
        pltpu.VMEM((2 * shard, group * rows), BF16),
        pltpu.VMEM((width, group * rows), F32),
        pltpu.VMEM((kv, n_span, part, group * width), F32),
        pltpu.VMEM((kv, n_col, shard, 2 * width), F32),
        pltpu.VMEM((kv, n_span, part, group * width), BF16),
        pltpu.VMEM((kv, n_span, part, group * width), BF16),
        pltpu.VMEM((2, shard, 2 * width), F32),
        pltpu.VMEM((kv, n_col, shard, 2 * width), BF16),
        pltpu.VMEM((kv, n_col, shard, 2 * width), BF16),
        pltpu.VMEM((kv, n_col, shard, 2 * width), BF16),
        pltpu.VMEM((kv, n_col, shard, 2 * width), BF16),
        dma((kv, n_sample)), dma((kv, n_col)), dma((kv, n_col)),
        dma((kv, n_col)), dma((kv, n_col)), dma((kv, n_col)), dma((kv, n_col)),
        dma((kv, n_span)), dma((kv, n_span)),
    ]
    return pl.pallas_call(
        functools.partial(body, n_col, n_span, kv, group),
        out_shape=out_shape,
        in_specs=[pl.BlockSpec(memory_space=pltpu.SMEM)] + [vmem] * 8,
        out_specs=(vmem,) * 5,
        scratch_shapes=scratch,
        compiler_params=pltpu.CompilerParams(
            collective_id=0, has_side_effects=True, vmem_limit_bytes=48 * 1024 * 1024),
        cost_estimate=pl.CostEstimate(
            flops=10 * heads * rows * (n_sample * shard + slice_key_rows.shape[1]) * width,
            bytes_accessed=8 * 1024 * 1024, transcendentals=heads * rows * n_sample * shard),
    )(lengths, queries, outputs, grad_out, log_norms,
      prompt_key_rows, prompt_value_rows, slice_key_rows, slice_value_rows)


def solution(mesh):
    in_specs = (
        P("sample", None, "kvhead"),
        P("sample", None, "kvhead"),
        P("sample", None, "kvhead"),
        P("sample", "kvhead", None),
        P("sample"),
        P(("sample", "span"), "kvhead"),
        P(("sample", "span"), "kvhead"),
        P("sample", "span", "kvhead"),
        P("sample", "span", "kvhead"),
    )
    out_specs = (
        P("sample", "span", "kvhead"),
        P(("sample", "span"), "kvhead"),
        P(("sample", "span"), "kvhead"),
        P("sample", "span", "kvhead"),
        P("sample", "span", "kvhead"),
    )
    return jax.shard_map(
        functools.partial(shards, mesh.shape["sample"], mesh.shape["span"]),
        mesh=mesh, in_specs=in_specs, out_specs=out_specs, check_vma=False)
```

time: 230 us -> 55.9 us (0.24)
  matrix products: 60.9 us -> 0 us
  waiting for transfers between devices: 59 us -> 0 us
  blocking collectives: 58.3 us -> 0 us
  Pallas kernels: 0 us -> 43.2 us
  local copies, waits for them, and re-layouts: 30.4 us -> 10.9 us
  between operations: 15 us -> 1.3 us
  other arithmetic: 5.29 us -> 0 us
    dot_general x15 -> x0, matrix products: 60.9 us -> none  [the longest x5 19.3 us: score_terms(): jnp.einsum('gqd,gkd->gqk', q_rows, key_heads, preferred_element_type=jnp....]
    reduce_scatter x2 -> x0, waiting for transfers between devices: 59 us -> none  [the longest x1 59 us: shards(): lax.psum_scatter(lax.fori_loop(0, lax.axis_size('sample') * shard_rows //...]
    all_gather x2 -> x0, blocking collectives: 58.3 us -> none  [the longest x1 29.5 us: shards(): lax.all_gather(prompt_value_rows, 'sample', axis=0, tiled=True)]
    pallas_call x0 -> x1, Pallas kernels: none -> 43.2 us  [shards(): pl.pallas_call(functools.partial(body, n_col, n_span, kv, group), out_sha...]
    reshape x9 -> x0, local copies, waits for them, and re-layouts: 4.16 us -> none  [the longest x1 2.79 us: shards(): query_total.reshape(kv_local, query_group_width, slice_rows, HEAD_WIDTH)]
    dynamic_slice x4 -> x0, local copies, waits for them, and re-layouts: 4.02 us -> none  [the longest x2 2.03 us: key_step(): lax.dynamic_slice_in_dim(gathered[1], offset, inner_rows, 0)]
    dynamic_update_slice x4 -> x0, local copies, waits for them, and re-layouts: 2.89 us -> none  [key_step(): lax.dynamic_update_slice_in_dim(state, jnp.concatenate([key_block, value_...]
    while x10 -> x0, local copies, waits for them, and re-layouts: 2.57 us -> none  [the longest x2 2.55 us: shards(): lax.fori_loop(0, lax.axis_size('sample') * shard_rows // inner_rows, key_...]
  transfers between devices with their start and end apart: 2 -> 0, of which waited for: 1 -> 0; matrix products, arithmetic and copies ran while one was open for 21% -> 0% of each run, Pallas kernels for 0% -> 0%
where the time goes in v1:
time: 55.9 us; the launch traced here: 55.4 us
  Pallas kernels  43.2 us (77%)
  local copies, waits for them, and re-layouts  10.9 us (19%)
  between operations  1.3 us (2%)
    pallas_call x1, Pallas kernels, shards(): pl.pallas_call(functools.partial(body, n_col, n_span, kv, group), out_sha...  43.2 us
    unnamed x20, local copies, waits for them, and re-layouts  10.9 us

profile of v1, /device:TPU:0, one launch (start us, length us, event | category | flops | bytes accessed | tf_op | source)
XLA Modules:
  0.0 55.4 jit_solution(4721861188275222932)
XLA Ops:
  1.3 0.7 %copy.14.refs_4_ = f32[1,14,256]{2,1,0:T(8,128)S(1)} copy(f32[1,14,256]{2,0,1:T(1,128)} %param.12) | data formatting | bytes 28672 | tf_op args[3]
  2.0 0.0 copy-start
  2.0 1.2 %copy-done = bf16[1,256,1792]{2,1,0:T(8,128)(2,1)S(1)} copy-done((bf16[1,256,1792]{2,1,0:T(8,128)(2,1)S(1)}, bf16[1,256,1792]{2,1,0:T(8,128)(2,1)}, u32[]{:S(2)}) %copy-start) | copy-done | bytes 917528
  3.2 0.0 copy-start.1
  3.2 1.2 %copy-done.1 = bf16[1,256,1792]{2,1,0:T(8,128)(2,1)S(1)} copy-done((bf16[1,256,1792]{2,1,0:T(8,128)(2,1)S(1)}, bf16[1,256,1792]{2,1,0:T(8,128)(2,1)}, u32[]{:S(2)}) %copy-start.1) | copy-done | bytes 917528
  4.4 0.0 copy-start.2
  4.4 1.2 %copy-done.2 = bf16[1,256,1792]{2,1,0:T(8,128)(2,1)S(1)} copy-done((bf16[1,256,1792]{2,1,0:T(8,128)(2,1)S(1)}, bf16[1,256,1792]{2,1,0:T(8,128)(2,1)}, u32[]{:S(2)}) %copy-start.2) | copy-done | bytes 917528
  5.5 0.0 copy-start.3
  5.5 0.8 %copy-done.3 = bf16[128,256]{1,0:T(8,128)(2,1)S(1)} copy-done((bf16[128,256]{1,0:T(8,128)(2,1)S(1)}, bf16[128,256]{1,0:T(8,128)(2,1)}, u32[]{:S(2)}) %copy-start.3) | copy-done | bytes 65560
  6.4 0.0 copy-start.4
  6.4 0.8 %copy-done.4 = bf16[128,256]{1,0:T(8,128)(2,1)S(1)} copy-done((bf16[128,256]{1,0:T(8,128)(2,1)S(1)}, bf16[128,256]{1,0:T(8,128)(2,1)}, u32[]{:S(2)}) %copy-start.4) | copy-done | bytes 65560
  7.2 0.0 copy-start.5
  7.2 0.8 %copy-done.5 = bf16[1,128,256]{2,1,0:T(8,128)(2,1)S(1)} copy-done((bf16[1,128,256]{2,1,0:T(8,128)(2,1)S(1)}, bf16[1,128,256]{2,1,0:T(8,128)(2,1)}, u32[]{:S(2)}) %copy-start.5) | copy-done | bytes 65560
  8.1 0.0 copy-start.6
  8.1 0.8 %copy-done.6 = bf16[1,128,256]{2,1,0:T(8,128)(2,1)S(1)} copy-done((bf16[1,128,256]{2,1,0:T(8,128)(2,1)S(1)}, bf16[1,128,256]{2,1,0:T(8,128)(2,1)}, u32[]{:S(2)}) %copy-start.6) | copy-done | bytes 65560
  8.9 43.2 %shard_map.128 = (bf16[1,128,1792]{2,1,0:T(8,128)(2,1)S(1)}, bf16[128,256]{1,0:T(8,128)(2,1)S(1)}, bf16[128,256]{1,0:T(8,128)(2,1)S(1)}, bf16[1,128,256]{2,1,0:T(8,128)(2,1)S(1)}, bf16[1,128,256]{2,1,0:T(8,128)(2,1)S(1)}) custom-call(s32[1]{0:T(128)S(6)} %copy.20.refs_0_, bf16[1,256,1792]{2,1,0:T(8,128)(2,1)S(1)} %copy-done, ...), custom_call_target="tpu_custom_call" | custom-call | flops 5284823040 | bytes 8388608 | tf_op jit(solution)/shard_map/pallas_call | solution.py:291
  52.1 0.8 %copy.21 = bf16[1,128,1792]{2,1,0:T(8,128)(2,1)} copy(bf16[1,128,1792]{2,1,0:T(8,128)(2,1)S(1)} %get-tuple-element.10) | data formatting | bytes 917504
  52.9 0.6 %copy.22 = bf16[128,256]{1,0:T(8,128)(2,1)} copy(bf16[128,256]{1,0:T(8,128)(2,1)S(1)} %get-tuple-element.11) | data formatting | bytes 131072
  53.5 0.6 %copy.23 = bf16[128,256]{1,0:T(8,128)(2,1)} copy(bf16[128,256]{1,0:T(8,128)(2,1)S(1)} %get-tuple-element.12) | data formatting | bytes 131072
  54.1 0.6 %copy.24 = bf16[1,128,256]{2,1,0:T(8,128)(2,1)} copy(bf16[1,128,256]{2,1,0:T(8,128)(2,1)S(1)} %get-tuple-element.13) | data formatting | bytes 131072
  54.8 0.6 %copy.25 = bf16[1,128,256]{2,1,0:T(8,128)(2,1)} copy(bf16[1,128,256]{2,1,0:T(8,128)(2,1)S(1)} %get-tuple-element.14) | data formatting | bytes 131072
Async XLA Ops:
  2.0 1.2 %copy-start = (bf16[1,256,1792]{2,1,0:T(8,128)(2,1)S(1)}, bf16[1,256,1792]{2,1,0:T(8,128)(2,1)}, u32[]{:S(2)}) copy-start(bf16[1,256,1792]{2,1,0:T(8,128)(2,1)} %refs_1_.1) | copy-start | bytes 2752516
  3.2 1.2 %copy-start.1 = (bf16[1,256,1792]{2,1,0:T(8,128)(2,1)S(1)}, bf16[1,256,1792]{2,1,0:T(8,128)(2,1)}, u32[]{:S(2)}) copy-start(bf16[1,256,1792]{2,1,0:T(8,128)(2,1)} %refs_2_.1) | copy-start | bytes 2752516
  4.4 1.2 %copy-start.2 = (bf16[1,256,1792]{2,1,0:T(8,128)(2,1)S(1)}, bf16[1,256,1792]{2,1,0:T(8,128)(2,1)}, u32[]{:S(2)}) copy-start(bf16[1,256,1792]{2,1,0:T(8,128)(2,1)} %refs_3_.1) | copy-start | bytes 2752516
  5.5 0.8 %copy-start.3 = (bf16[128,256]{1,0:T(8,128)(2,1)S(1)}, bf16[128,256]{1,0:T(8,128)(2,1)}, u32[]{:S(2)}) copy-start(bf16[128,256]{1,0:T(8,128)(2,1)} %refs_5_.1) | copy-start | bytes 196612
  6.4 0.8 %copy-start.4 = (bf16[128,256]{1,0:T(8,128)(2,1)S(1)}, bf16[128,256]{1,0:T(8,128)(2,1)}, u32[]{:S(2)}) copy-start(bf16[128,256]{1,0:T(8,128)(2,1)} %refs_6_.1) | copy-start | bytes 196612
  7.2 0.8 %copy-start.5 = (bf16[1,128,256]{2,1,0:T(8,128)(2,1)S(1)}, bf16[1,128,256]{2,1,0:T(8,128)(2,1)}, u32[]{:S(2)}) copy-start(bf16[1,128,256]{2,1,0:T(8,128)(2,1)} %refs_7_.1) | copy-start | bytes 196612
  8.1 0.8 %copy-start.6 = (bf16[1,128,256]{2,1,0:T(8,128)(2,1)S(1)}, bf16[1,128,256]{2,1,0:T(8,128)(2,1)}, u32[]{:S(2)}) copy-start(bf16[1,128,256]{2,1,0:T(8,128)(2,1)} %refs_8_.1) | copy-start | bytes 196612

commit v2 on v1

--- a/solution.py
+++ b/solution.py
@@ -29,14 +29,15 @@
 
 def kernel(
     n_col, n_span, kv, group,
-    len_ref, q_ref, o_ref, g_ref, lse_ref, pk_ref, pv_ref, sk_ref, sv_ref,
+    len_ref, q_hbm, o_hbm, g_hbm, lse_hbm, pk_hbm, pv_hbm, sk_hbm, sv_hbm,
     dq_ref, dkp_ref, dvp_ref, dks_ref, dvs_ref,
     qst, gst, lse2, delta, kv_all, probs, grads, dqt, dqf, dqs, dqr,
     own, ysend, yrecv, zsend, zrecv,
+    q_ref, o_ref, g_ref, lse_ref, sk_ref, sv_ref, load_sem,
     kv_recv, kvz_send, kvy_send, y_ssem, y_rsem, z_ssem, z_rsem, q_ssem, q_rsem,
 ):
-    rows = q_ref.shape[1]
-    shard = pk_ref.shape[0]
+    rows = q_hbm.shape[1]
+    shard = pk_hbm.shape[0]
     width = HEAD_WIDTH
     part = rows // n_span
     scale = 1.0 / math.sqrt(HEAD_WIDTH)
@@ -54,6 +55,16 @@
 
     partner = at_sample(col, 1 - side)
 
+    loads = []
+    for g in range(kv):
+        lanes = slice(g * width, (g + 1) * width)
+        for n, source in enumerate((pk_hbm, pv_hbm)):
+            target = kv_all.at[g, sample, :, n * width:(n + 1) * width]
+            loads.append(pltpu.make_async_copy(source.at[:, lanes], target, load_sem.at[len(loads)]))
+    for source, target in ((q_hbm, q_ref), (g_hbm, g_ref), (o_hbm, o_ref), (lse_hbm, lse_ref),
+                           (sk_hbm, sk_ref), (sv_hbm, sv_ref)):
+        loads.append(pltpu.make_async_copy(source, target, load_sem.at[len(loads)]))
+
     barrier = pltpu.get_barrier_semaphore()
     for d in range(1, n_col):
         pl.semaphore_signal(barrier, inc=1, device_id=at_sample(column(d), side), device_id_type=MESH)
@@ -62,10 +73,10 @@
         peer = (sample, lax.rem(span + e, n_span), core)
         pl.semaphore_signal(barrier, inc=1, device_id=peer, device_id_type=MESH)
 
-    for g in range(kv):
-        lanes = slice(g * width, (g + 1) * width)
-        kv_all[g, sample, :, 0:width] = pk_ref[:, lanes]
-        kv_all[g, sample, :, width:2 * width] = pv_ref[:, lanes]
+    for load in loads:
+        load.start()
+    for load in loads[:2 * kv]:
+        load.wait()
     pl.semaphore_wait(barrier, n_col + n_span - 1)
 
     def z_copy(g, d):
@@ -115,8 +126,9 @@
             z_copy(g, d).start()
         y_copy(g, 0).start()
 
+    for load in loads[2 * kv:]:
+        load.wait()
     live = lax.broadcasted_iota(jnp.int32, (rows, width), 0) < len_ref[0]
-    lse2[...] = lse_ref[0] * LOG2E
     for h in range(kv * group):
         lanes = slice(h * width, (h + 1) * width)
         g, i = divmod(h, group)
@@ -125,6 +137,7 @@
         grad = jnp.where(live, g_ref[0, :, lanes].astype(F32), 0.0)
         gst[g, span_rows, :] = grad.astype(BF16)
         prod = grad * o_ref[0, :, lanes].astype(F32)
+        lse2[h:h + 1, :] = lse_ref[h] * LOG2E
         delta[h:h + 1, :] = jnp.sum(prod.T, axis=0, keepdims=True)
 
     def block(g, keys, values, mask, first):
@@ -142,9 +155,9 @@
         low = grads[0:count, :]
         term = dot_tn(keys, low)
         if first:
-            dqt[...] = term
+            dqt[g] = term
         else:
-            dqt[...] += term
+            dqt[g] += term
         key_grad = dot_nn(low, qst[g]) * scale
         value_grad = dot_nn(probs[0:count, :], gst[g])
         return key_grad, value_grad
@@ -179,38 +192,32 @@
         key_grad, value_grad = block(g, sk_ref[0, :, lanes], sv_ref[0, :, lanes], visible, True)
         dks_ref[0, :, lanes] = key_grad.astype(BF16)
         dvs_ref[0, :, lanes] = value_grad.astype(BF16)
-        if g == 0:
-            forward(g, 1)
-
+        for k in range(1, n_col):
+            forward(g, k)
+
+    for g in range(kv):
         def step(k, carry, g=g):
-            if g == 0:
-                @pl.when(k + 1 < n_col)
-                def _():
-                    forward(g, k + 1)
             wait_block(g, column(k) * 2 + 1 - side)
             zhold[g, k] = column_block(g, k)
 
-            @pl.when(k >= 2)
+            @pl.when(k >= 3)
             def _():
-                z_finish(g, k - 1)
+                z_finish(g, k - 2)
             return carry
 
         lax.fori_loop(1, n_col, step, 0)
-        for later in range(1, kv):
-            if g == 0:
-                for k in range(1, n_col):
-                    forward(later, k)
         wait_block(g, column(0) * 2 + 1 - side)
         zhold[g, 0] = column_block(g, 0)
-        z_finish(g, n_col - 1)
         for i in range(group):
             lanes_i = slice(i * width, (i + 1) * width)
-            part_sum = dqt[:, i * rows:(i + 1) * rows].T * scale
+            part_sum = dqt[g, :, i * rows:(i + 1) * rows].T * scale
             whole = part_sum.reshape(n_span, part, width)
             dq_acc[g, :, :, lanes_i] = whole
             dqs[g, :, :, lanes_i] = whole.astype(BF16)
         for e in range(1, n_span):
             query_copy(g, e).start()
+        for k in range(max(1, n_col - 2), n_col):
+            z_finish(g, k)
 
     for g in range(kv):
         lanes = slice(g * width, (g + 1) * width)
@@ -274,7 +281,7 @@
         pltpu.VMEM((kv, n_sample, shard, 2 * width), BF16),
         pltpu.VMEM((2 * shard, group * rows), BF16),
         pltpu.VMEM((2 * shard, group * rows), BF16),
-        pltpu.VMEM((width, group * rows), F32),
+        pltpu.VMEM((kv, width, group * rows), F32),
         pltpu.VMEM((kv, n_span, part, group * width), F32),
         pltpu.VMEM((kv, n_col, shard, 2 * width), F32),
         pltpu.VMEM((kv, n_span, part, group * width), BF16),
@@ -284,6 +291,13 @@
         pltpu.VMEM((kv, n_col, shard, 2 * width), BF16),
         pltpu.VMEM((kv, n_col, shard, 2 * width), BF16),
         pltpu.VMEM((kv, n_col, shard, 2 * width), BF16),
+        pltpu.VMEM(queries.shape, BF16),
+        pltpu.VMEM(queries.shape, BF16),
+        pltpu.VMEM(queries.shape, BF16),
+        pltpu.VMEM((heads, 1, rows), F32),
+        pltpu.VMEM(slice_key_rows.shape, BF16),
+        pltpu.VMEM(slice_key_rows.shape, BF16),
+        dma((2 * kv + 6,)),
         dma((kv, n_sample)), dma((kv, n_col)), dma((kv, n_col)),
         dma((kv, n_col)), dma((kv, n_col)), dma((kv, n_col)), dma((kv, n_col)),
         dma((kv, n_span)), dma((kv, n_span)),
@@ -291,15 +305,15 @@
     return pl.pallas_call(
         functools.partial(body, n_col, n_span, kv, group),
         out_shape=out_shape,
-        in_specs=[pl.BlockSpec(memory_space=pltpu.SMEM)] + [vmem] * 8,
+        in_specs=[pl.BlockSpec(memory_space=pltpu.SMEM)] + [pl.BlockSpec(memory_space=pltpu.HBM)] * 8,
         out_specs=(vmem,) * 5,
         scratch_shapes=scratch,
         compiler_params=pltpu.CompilerParams(
-            collective_id=0, has_side_effects=True, vmem_limit_bytes=48 * 1024 * 1024),
+            collective_id=0, has_side_effects=True, vmem_limit_bytes=60 * 1024 * 1024),
         cost_estimate=pl.CostEstimate(
             flops=10 * heads * rows * (n_sample * shard + slice_key_rows.shape[1]) * width,
             bytes_accessed=8 * 1024 * 1024, transcendentals=heads * rows * n_sample * shard),
-    )(lengths, queries, outputs, grad_out, log_norms,
+    )(lengths, queries, outputs, grad_out, log_norms.reshape(heads, 1, rows),
       prompt_key_rows, prompt_value_rows, slice_key_rows, slice_value_rows)
 
 

time: 55.9 us -> 47.9 us (0.86)
  local copies, waits for them, and re-layouts: 10.9 us -> 5.07 us
  Pallas kernels: 43.2 us -> 41.2 us
    unnamed x20 -> x13, local copies, waits for them, and re-layouts: 10.9 us -> 5.07 us
    pallas_call x1, Pallas kernels: 43.2 us -> 41.2 us  [shards(): pl.pallas_call(functools.partial(body, n_col, n_span, kv, group), out_sha...]
where the time goes in v2:
time: 47.9 us; the launch traced here: 47.6 us
  Pallas kernels  41.2 us (86%)
  local copies, waits for them, and re-layouts  5.07 us (11%)
  between operations  1.3 us (3%)
    pallas_call x1, Pallas kernels, shards(): pl.pallas_call(functools.partial(body, n_col, n_span, kv, group), out_sha...  41.2 us
    unnamed x13, local copies, waits for them, and re-layouts  5.07 us

profile of v2, /device:TPU:0, one launch (start us, length us, event | category | flops | bytes accessed | tf_op | source)
XLA Modules:
  0.0 47.6 jit_solution(16659504793882517842)
XLA Ops:
  1.3 41.2 %shard_map.128 = (bf16[1,128,1792]{2,1,0:T(8,128)(2,1)}, bf16[128,256]{1,0:T(8,128)(2,1)}, bf16[128,256]{1,0:T(8,128)(2,1)}, bf16[1,128,256]{2,1,0:T(8,128)(2,1)}, bf16[1,128,256]{2,1,0:T(8,128)(2,1)}) custom-call(s32[1]{0:T(128)S(6)} %copy.19.refs_0_, bf16[1,256,1792]{2,1,0:T(8,128)(2,1)} %refs_1_.1, bf16[1,256,1792]{2,1,0:T(8,128)(2,1)} %refs_2_.1, ...), custom_call_target="tpu_custom_call" | custom-call | flops 5284823040 | bytes 8388608 | tf_op jit(solution)/shard_map/pallas_call | solution.py:305
  42.5 0.0 copy-start.3
  42.5 1.8 %copy.20 = bf16[1,128,1792]{2,1,0:T(8,128)(2,1)} copy(bf16[1,128,1792]{2,1,0:T(8,128)(2,1)} %get-tuple-element.10) | data formatting | bytes 917504
  44.4 0.0 copy-done.3
  44.4 0.0 copy-start.2
  44.4 0.6 %copy.21 = bf16[128,256]{1,0:T(8,128)(2,1)} copy(bf16[128,256]{1,0:T(8,128)(2,1)S(1)} %copy-done.3) | data formatting | bytes 131072
  45.0 0.2 copy-done.2
  45.3 0.0 copy-start.1
  45.3 0.6 %copy.22 = bf16[128,256]{1,0:T(8,128)(2,1)} copy(bf16[128,256]{1,0:T(8,128)(2,1)S(1)} %copy-done.2) | data formatting | bytes 131072
  45.9 0.2 copy-done.1
  46.1 0.0 copy-start
  46.1 0.6 %copy.23 = bf16[1,128,256]{2,1,0:T(8,128)(2,1)} copy(bf16[1,128,256]{2,1,0:T(8,128)(2,1)S(1)} %copy-done.1) | data formatting | bytes 131072
  46.7 0.2 copy-done
  47.0 0.6 %copy.24 = bf16[1,128,256]{2,1,0:T(8,128)(2,1)} copy(bf16[1,128,256]{2,1,0:T(8,128)(2,1)S(1)} %copy-done) | data formatting | bytes 131072
Async XLA Ops:
  42.5 1.9 %copy-start.3 = (bf16[128,256]{1,0:T(8,128)(2,1)S(1)}, bf16[128,256]{1,0:T(8,128)(2,1)}, u32[]{:S(2)}) copy-start(bf16[128,256]{1,0:T(8,128)(2,1)} %get-tuple-element.11) | copy-start | bytes 196612
  44.4 0.9 %copy-start.2 = (bf16[128,256]{1,0:T(8,128)(2,1)S(1)}, bf16[128,256]{1,0:T(8,128)(2,1)}, u32[]{:S(2)}) copy-start(bf16[128,256]{1,0:T(8,128)(2,1)} %get-tuple-element.12) | copy-start | bytes 196612
  45.3 0.9 %copy-start.1 = (bf16[1,128,256]{2,1,0:T(8,128)(2,1)S(1)}, bf16[1,128,256]{2,1,0:T(8,128)(2,1)}, u32[]{:S(2)}) copy-start(bf16[1,128,256]{2,1,0:T(8,128)(2,1)} %get-tuple-element.13) | copy-start | bytes 196612
  46.1 0.9 %copy-start = (bf16[1,128,256]{2,1,0:T(8,128)(2,1)S(1)}, bf16[1,128,256]{2,1,0:T(8,128)(2,1)}, u32[]{:S(2)}) copy-start(bf16[1,128,256]{2,1,0:T(8,128)(2,1)} %get-tuple-element.14) | copy-start | bytes 196612
